TPU v7x, 512 devices: a whole 4x8x8 slice. The times are simulated.
512 devices in a mesh: cfg: 64 (over y, x, core), tp: 8 (over z).
Axes of the slice: x: 4, y: 8, z: 8, core: 2. Of those that a mesh axis runs over, the one named last changes fastest.
Arguments:
- pool: bfloat16 [64, 192, 8192], P('cfg', None, 'tp'), may hold values from -6 to 6
- base_run: int32 [1], replicated, may hold values from 0 to 63
- gain: bfloat16 [8192], replicated, may hold values from 0.099609375 to 1.8984375
- w_key: bfloat16 [8192, 1024], P(None, 'tp'), may hold values from -0.0625 to 0.0625
- w_value: bfloat16 [8192, 1024], P(None, 'tp'), may hold values from -0.0625 to 0.0625
- w_query: bfloat16 [8192, 8192], P('cfg', 'tp'), may hold values from -0.0625 to 0.0625
- src_pos: int32 [192, 64, 2], P(None, 'cfg'), may hold values from 0 to 191
- dst_pos: int32 [192, 64, 2], P('cfg'), may hold values from 0 to 187, as said below
- counts: int32 [192, 64], P('cfg'), may hold values from 0 to 2
Outputs:
- attended: bfloat16 [192, 4, 8192], P('cfg', None, 'tp')
- keys: bfloat16 [192, 192, 1024], P('cfg', None, 'tp')
- values: bfloat16 [192, 192, 1024], P('cfg', None, 'tp')
Inputs may be any that keep to these rules, and one draw needn't show every extreme that they name: `dst_pos`: within one config all 128 entries differ and lie below 188. `counts`: slots of config c and source run s in use, the first ones of the 2.
All inputs are finite; a program needn't handle non-finite values.
Results may differ from a plain program's by a relative error of at most 0.023.
Values may be sent and summed in bfloat16 or wider, within the bound.
A program may use at most 64 MiB of HBM per device.

v0:
```python
import math
import jax
import jax.numpy as jnp
from jax import lax
from jax.sharding import PartitionSpec as P

D = 8192
HD = 128
PROBE = 4
rope_base = 500000.0
epsilon = 1e-05


def spread(value, axis, source):
    kept = jnp.where(lax.axis_index(axis) == source, value, 0).astype(value.dtype)
    return lax.psum(kept, axis)


def rotate(tensor, positions):
    half_dim = tensor.shape[-1] // 2
    inverse_freq = jnp.exp(
        jnp.arange(half_dim, dtype=jnp.float32) * (-2.0 * math.log(rope_base) / tensor.shape[-1])
    )
    angles = positions.astype(jnp.float32)[:, None] * inverse_freq[None, :]
    cosine = jnp.cos(angles)[:, None, :]
    sine_vals = jnp.sin(angles)[:, None, :]
    lower_half = tensor[..., :half_dim]
    upper_half = tensor[..., half_dim:]
    return jnp.concatenate(
        [
            lower_half * cosine - upper_half * sine_vals,
            upper_half * cosine + lower_half * sine_vals,
        ],
        axis=-1,
    )


def body(pool, base_run, gain, w_key, w_value, w_query, src_pos, dst_pos, counts):
    length = pool.shape[1]
    local_cfg = dst_pos.shape[0]
    slot_count = dst_pos.shape[1] * dst_pos.shape[2]
    key_cols = w_key.shape[1]
    in_use = jnp.arange(dst_pos.shape[2], dtype=jnp.int32)[None, None, :] < counts[:, :, None]
    targets = jnp.where(in_use, dst_pos, length).reshape(local_cfg, slot_count)
    onehot = targets[:, :, None] == jnp.arange(length, dtype=jnp.int32)[None, None, :]
    covered = jnp.any(onehot, axis=1)
    base_rows = spread(pool[0], "cfg", base_run[0])
    picked = jnp.take(pool[0], src_pos[:, 0, :], axis=0)[:, None]
    arrived = lax.all_to_all(picked, "cfg", split_axis=0, concat_axis=1, tiled=True)
    arrived = arrived.reshape(local_cfg, slot_count, arrived.shape[-1])
    spliced = jnp.einsum(
        "csp,csd->cpd", onehot.astype(jnp.bfloat16), arrived, preferred_element_type=jnp.float32
    )
    patched = jnp.where(covered[:, :, None], spliced, base_rows[None].astype(jnp.float32)).astype(
        jnp.bfloat16
    )
    rows = patched.reshape(local_cfg * length, patched.shape[-1])
    gains = gain.astype(jnp.float32)
    widened = lax.all_gather(rows, "tp", axis=1, tiled=True).astype(jnp.float32)
    normed = (widened * gains[None, :]).astype(jnp.bfloat16)
    keys_acc = jnp.dot(normed, w_key, preferred_element_type=jnp.float32)
    values_acc = jnp.dot(normed, w_value, preferred_element_type=jnp.float32)
    squares = jnp.sum(widened * widened, axis=1)
    probe_rows = normed[length - PROBE : length]
    keys_acc, values_acc, squares, probe_rows = (keys_acc, values_acc, squares, probe_rows)
    scales = lax.rsqrt(squares / D + epsilon)
    key_raw = (scales[:, None] * keys_acc).reshape(local_cfg, length, key_cols)
    value_raw = (scales[:, None] * values_acc).reshape(local_cfg, length, key_cols)
    probe_scales = scales[length - PROBE : length]
    slice_rows = w_query.shape[0]
    probe_part = lax.dynamic_slice_in_dim(
        probe_rows, lax.axis_index("cfg") * slice_rows, slice_rows, 1
    )
    partial_value = jnp.dot(probe_part, w_query, preferred_element_type=jnp.float32)
    query_total = lax.psum(partial_value, "cfg")
    heads_dev = w_query.shape[1] // HD
    kv_dev = key_cols // HD
    group_size = heads_dev // kv_dev
    positions = jnp.arange(length, dtype=jnp.int32)
    probe_pos = length - PROBE + jnp.arange(PROBE, dtype=jnp.int32)
    queries = rotate(
        (probe_scales[:, None] * query_total).reshape(PROBE, heads_dev, HD), probe_pos
    ).astype(jnp.bfloat16)
    keys_out = rotate(key_raw.reshape(local_cfg, length, kv_dev, HD), positions).astype(
        jnp.bfloat16
    )
    values_out = value_raw.astype(jnp.bfloat16)
    query_groups = queries.reshape(PROBE, kv_dev, group_size, HD)
    value_heads = values_out.reshape(local_cfg, length, kv_dev, HD)
    scores = jnp.einsum(
        "pkgh,cskh->cpkgs", query_groups, keys_out, preferred_element_type=jnp.float32
    ) * HD ** (-0.5)
    causal = positions[None, :] <= probe_pos[:, None]
    scores = jnp.where(causal[None, :, None, None, :], scores, -1e30)
    probs_b = jax.nn.softmax(scores, axis=-1).astype(jnp.bfloat16)
    attended = jnp.einsum(
        "cpkgs,cskh->cpkgh", probs_b, value_heads, preferred_element_type=jnp.float32
    )
    attended = attended.astype(jnp.bfloat16).reshape(local_cfg, PROBE, heads_dev * HD)
    return (attended, keys_out.reshape(local_cfg, length, key_cols), values_out)


def solution(mesh):
    placed = (
        P("cfg", None, "tp"),
        P(),
        P(),
        P(None, "tp"),
        P(None, "tp"),
        P("cfg", "tp"),
        P(None, "cfg", None),
        P("cfg", None, None),
        P("cfg", None),
    )
    return jax.shard_map(
        body,
        mesh=mesh,
        in_specs=placed,
        out_specs=(P("cfg", None, "tp"), P("cfg", None, "tp"), P("cfg", None, "tp")),
        check_vma=False,
    )
```

profile of v0, /device:TPU:32, one launch (start us, length us, event | category | flops | bytes accessed | tf_op | source)
XLA Modules:
  0.0 618.3 jit_solution(13707132915547980617)
XLA Ops:
  7.2 0.0 copy-start
  7.2 0.0 copy-start.1
  7.2 0.0 copy-start.5
  7.2 0.0 copy-start.6
  7.2 0.8 compare_select_fusion
  8.0 0.7 compare_and_fusion
  8.7 0.1 copy.19
  8.9 0.1 reshape.268
  9.0 0.0 copy-start.4
  9.0 3.8 gather_fusion
  12.9 1.2 gather.7
  14.0 0.2 copy.18
  14.2 2.7 broadcast_select_fusion
  16.9 10.3 %all-to-all-start = ((bf16[192,1,2,1024]{3,2,1,0:T(2,128)(2,1)}), bf16[192,1,2,1024]{3,2,1,0:T(2,128)(2,1)S(1)}, u32[]{:S(2)}, u32[]{:S(2)}) async-start(bf16[192,1,2,1024]{3,2,1,0:T(2,128)(2,1)} %broadcast_select_fusion), calls=%async_computation | async-start | bytes 1572864 | tf_op jit(solution)/shard_map/all_to_all | solution.py:49
  27.2 0.0 all-reduce.2.cloned.1.call-start
  27.9 0.0 copy-done.1
  27.9 0.8 broadcast_select_fusion.1
  28.7 0.0 all-reduce.2.cloned.1.call-update
  28.7 0.0 all-gather.2.cloned.1.call-start
  28.8 0.0 copy-done.5
  28.8 0.0 copy-done.6
  28.8 0.1 copy.17
  28.9 0.1 eq.18
  29.1 0.2 fusion.6
  29.3 18.0 %all-to-all-done = bf16[192,1,2,1024]{3,2,1,0:T(2,128)(2,1)S(1)} async-done(((bf16[192,1,2,1024]{3,2,1,0:T(2,128)(2,1)}), bf16[192,1,2,1024]{3,2,1,0:T(2,128)(2,1)S(1)}, u32[]{:S(2)}, u32[]{:S(2)}) %all-to-all-start) | async-done | bytes 786464 | tf_op jit(solution)/shard_map/all_to_all | solution.py:49
  47.3 1.4 copy.21
  48.7 2.3 reshape.261
  51.0 174.9 %all-reduce.2.cloned.1.call-done = bf16[192,1024]{1,0:T(8,128)(2,1)} async-done(((bf16[192,1024]{1,0:T(8,128)(2,1)}), bf16[192,1024]{1,0:T(8,128)(2,1)}) %all-reduce.2.cloned.1.call-update) | async-done | bytes 393232 | tf_op jit(solution)/shard_map/psum | solution.py:16
  225.8 2.5 select_convert_fusion
  228.3 0.0 all-gather.2.cloned.1.call-update
  228.3 0.0 copy-done.4
  228.4 0.1 iota_compare_fusion.2
  228.5 0.1 multiply_cosine_fusion.1
  228.6 0.4 multiply_cosine_fusion
  229.0 107.6 %all-gather.2.cloned.1.call-done = bf16[576,8192]{1,0:T(8,128)(2,1)} async-done(((bf16[576,1024]{1,0:T(8,128)(2,1)}), bf16[576,8192]{1,0:T(8,128)(2,1)}) %all-gather.2.cloned.1.call-update) | async-done | bytes 9437200 | tf_op jit(solution)/shard_map/all_gather | solution.py:59
  336.6 11.2 %fusion = (f32[576]{0:T(1024)S(1)}, bf16[576,8192]{1,0:T(8,128)(2,1)}) fusion(bf16[576,8192]{1,0:T(8,128)(2,1)} %all-gather.2.cloned.1.call-done, f32[8192]{0:T(1024)S(1)} %convert_element_type.76), kind=kLoop, calls=%fused_computation.3 | loop fusion | flops 23592384 | bytes 18909440 | tf_op jit(solution)/shard_map/reduce_sum | solution.py:63
  347.8 0.0 copy-start.3
  347.8 1.0 slice.28
  348.8 0.1 slice.20
  348.9 0.0 copy-done
  348.9 5.2 convolution_multiply_fusion
  354.0 0.0 copy-done.3
  354.0 0.1 fusion.16
  354.2 248.4 %psum.15 = f32[4,1024]{1,0:T(4,128)S(1)} all-reduce(f32[4,1024]{1,0:T(4,128)S(1)} %fusion.16), channel_id=1, replica_groups=mesh['cfg'=64,'tp'=8] {'cfg'}, use_global_device_ids=true, to_apply=%region_3.4 | all-reduce | flops 4096 | bytes 32768 | tf_op jit(solution)/shard_map/psum | solution.py:75
  602.6 0.1 multiply_bitcast_fusion
  602.7 6.9 %fusion.2 = bf16[576,128]{1,0:T(8,128)(2,1)S(1)} fusion(bf16[576,8192]{1,0:T(8,128)(2,1)} %get-tuple-element.4, bf16[8192,128]{1,0:T(8,128)(2,1)} %param.13, f32[576]{0:T(1024)S(1)} %add_rsqrt_fusion), kind=kOutput, calls=%fused_computation.9 | convolution fusion | flops 1208107008 | bytes 11684096 | tf_op jit(solution)/shard_map/dot_general | solution.py:62
  609.6 0.0 copy-start.7
  609.7 0.2 fusion.7
  609.8 0.1 pad_maximum_fusion
  609.9 0.0 copy-start.2
  610.0 0.1 subtract_convert_fusion.1
  610.0 0.3 fusion.21
  610.4 0.2 fusion.11
  610.6 0.2 fusion.5
  610.8 0.6 reshape.265
  611.4 0.0 copy-done.7
  611.4 0.0 copy-done.2
  (9 shorter events, 0.0 us)
Async XLA Ops:
  7.2 341.7 %copy-start = (bf16[8192,128]{1,0:T(8,128)(2,1)S(1)}, bf16[8192,128]{1,0:T(8,128)(2,1)}, u32[]{:S(2)}) copy-start(bf16[8192,128]{1,0:T(8,128)(2,1)} %param.12) | copy-start | bytes 6291460
  7.2 20.7 %copy-start.1 = (bf16[1,192,1024]{2,1,0:T(8,128)(2,1)S(1)}, bf16[1,192,1024]{2,1,0:T(8,128)(2,1)}, u32[]{:S(2)}) copy-start(bf16[1,192,1024]{2,1,0:T(8,128)(2,1)} %param.9) | copy-start | bytes 1179652
  7.2 21.6 %copy-start.5 = (s32[3,64,2]{1,2,0:T(2,128)S(1)}, s32[3,64,2]{1,2,0:T(2,128)}, u32[]{:S(2)}) copy-start(s32[3,64,2]{1,2,0:T(2,128)} %param.16) | copy-start | bytes 4612
  7.2 21.6 %copy-start.6 = (s32[3,64]{1,0:T(4,128)S(1)}, s32[3,64]{1,0:T(4,128)}, u32[]{:S(2)}) copy-start(s32[3,64]{1,0:T(4,128)} %param.17) | copy-start | bytes 2308
  9.0 219.3 %copy-start.4 = (bf16[8192]{0:T(1024)(128)(2,1)S(1)}, bf16[8192]{0:T(1024)(128)(2,1)}, u32[]{:S(2)}) copy-start(bf16[8192]{0:T(1024)(128)(2,1)} %param.11) | copy-start | bytes 49156
  16.9 30.4 %all-to-all-start = ((bf16[192,1,2,1024]{3,2,1,0:T(2,128)(2,1)}), bf16[192,1,2,1024]{3,2,1,0:T(2,128)(2,1)S(1)}, u32[]{:S(2)}, u32[]{:S(2)}) async-start(bf16[192,1,2,1024]{3,2,1,0:T(2,128)(2,1)} %broadcast_select_fusion), calls=%async_computation | async-start | bytes 1572864 | tf_op jit(solution)/shard_map/all_to_all | solution.py:49
  27.2 198.6 %all-reduce.2.cloned.1.call-start = ((), (), s32[]{:S(2)}) async-start(), calls=%async_computation.1 | async-start | bytes 786432 | tf_op jit(solution)/shard_map/psum | solution.py:16
  28.7 307.9 %all-gather.2.cloned.1.call-start = ((), (), s32[]{:S(2)}) async-start(), calls=%async_computation.2 | async-start | bytes 10616832 | tf_op jit(solution)/shard_map/all_gather | solution.py:59
  347.8 6.3 %copy-start.3 = (bf16[128,1024]{1,0:T(8,128)(2,1)S(1)}, bf16[128,1024]{1,0:T(8,128)(2,1)}, u32[]{:S(2)}) copy-start(bf16[128,1024]{1,0:T(8,128)(2,1)} %param.14) | copy-start | bytes 786436
  609.6 1.8 copy-start.7
  609.9 1.5 copy-start.2
Sparse Core Ops, SparseCore 0:
  31.5 194.2 all-reduce.1
  228.4 108.1 all-gather.1
where the time goes:
time: 619 us; the launch traced here: 618 us
  waiting for transfers between devices  300 us (48%)
  blocking collectives  248 us (40%)
  other arithmetic  17.6 us (3%)
  matrix products  15.3 us (2%)
  between operations  14.9 us (2%)
  local copies, waits for them, and re-layouts  11.1 us (2%)
  starting transfers between devices  10.4 us (2%)
    psum x1, blocking collectives, body(): query_total = lax.psum(partial_value, 'cfg')  248 us
    psum x1, waiting for transfers between devices, spread(): return lax.psum(kept, axis)  175 us
    all_gather x1, waiting for transfers between devices, body(): widened = lax.all_gather(rows, 'tp', axis=1, tiled=True).astype(jnp.float32)  108 us
    all_to_all x1, waiting for transfers between devices, body(): lax.all_to_all(picked, 'cfg', split_axis=0, concat_axis=1, tiled=True)  18 us
  transfers between devices with their start and end apart: 3, of which 3 were waited for; matrix products, arithmetic and copies ran while one was open for 1% of the time, Pallas kernels for 0%

commit v1 on v0

--- a/solution.py
+++ b/solution.py
@@ -56,7 +56,9 @@
     )
     rows = patched.reshape(local_cfg * length, patched.shape[-1])
     gains = gain.astype(jnp.float32)
-    widened = lax.all_gather(rows, "tp", axis=1, tiled=True).astype(jnp.float32)
+    widened = jnp.concatenate(
+        lax.all_to_all(jnp.stack([rows] * lax.axis_size("tp")), "tp", 0, 0), axis=1
+    ).astype(jnp.float32)
     normed = (widened * gains[None, :]).astype(jnp.bfloat16)
     keys_acc = jnp.dot(normed, w_key, preferred_element_type=jnp.float32)
     values_acc = jnp.dot(normed, w_value, preferred_element_type=jnp.float32)

time: 619 us -> 750 us (1.21)
  waiting for transfers between devices: 300 us -> 401 us
  local copies, waits for them, and re-layouts: 11.1 us -> 26.9 us
  other arithmetic: 17.6 us -> 27.1 us
    all_to_all x0 -> x1, waiting for transfers between devices: none -> 208 us  [body(): lax.all_to_all(jnp.stack([rows] * lax.axis_size('tp')), 'tp', 0, 0)]
    all_gather x1 -> x0, waiting for transfers between devices: 108 us -> none  [body(): widened = lax.all_gather(rows, 'tp', axis=1, tiled=True).astype(jnp.float32)]
    unnamed x1 -> x2, other arithmetic: 0.08 us -> 12.7 us
    convert_element_type x0 -> x1, local copies, waits for them, and re-layouts: none -> 7.82 us  [body(): widened = jnp.concatenate(lax.all_to_all(jnp.stack([rows] * lax.axis_size...]
    all_to_all x0 -> x1, starting transfers between devices: none -> 7.51 us  [body(): lax.all_to_all(jnp.stack([rows] * lax.axis_size('tp')), 'tp', 0, 0)]
where the time goes in v1:
time: 750 us; the launch traced here: 749 us
  waiting for transfers between devices  401 us (53%)
  blocking collectives  250 us (33%)
  other arithmetic  27.1 us (4%)
  local copies, waits for them, and re-layouts  26.9 us (4%)
  starting transfers between devices  17.9 us (2%)
  between operations  14.9 us (2%)
  matrix products  11.2 us (1%)
    psum x1, blocking collectives, body(): query_total = lax.psum(partial_value, 'cfg')  250 us
    all_to_all x1, waiting for transfers between devices, body(): lax.all_to_all(jnp.stack([rows] * lax.axis_size('tp')), 'tp', 0, 0)  208 us
    psum x1, waiting for transfers between devices, spread(): return lax.psum(kept, axis)  175 us
    all_to_all x1, waiting for transfers between devices, body(): lax.all_to_all(picked, 'cfg', split_axis=0, concat_axis=1, tiled=True)  18 us
  transfers between devices with their start and end apart: 3, of which 3 were waited for; matrix products, arithmetic and copies ran while one was open for 1% of the time, Pallas kernels for 0%

profile of v1, /device:TPU:32, one launch (start us, length us, event | category | flops | bytes accessed | tf_op | source)
XLA Modules:
  0.0 749.2 jit_solution(9854432013818762748)
XLA Ops:
  7.2 0.0 copy-start
  7.2 0.0 copy-start.1
  7.2 0.0 copy-start.8
  7.2 0.0 copy-start.7
  7.2 0.8 compare_and_fusion
  8.1 0.7 compare_select_fusion
  8.7 0.2 copy.18
  8.9 0.1 copy.19
  9.0 0.1 reshape.271
  9.2 3.8 gather_fusion
  13.0 1.2 gather.7
  14.2 2.7 broadcast_select_fusion
  16.9 10.3 %all-to-all-start = ((bf16[192,1,2,1024]{3,2,1,0:T(2,128)(2,1)}), bf16[192,1,2,1024]{3,2,1,0:T(2,128)(2,1)S(1)}, u32[]{:S(2)}, u32[]{:S(2)}) async-start(bf16[192,1,2,1024]{3,2,1,0:T(2,128)(2,1)} %broadcast_select_fusion), calls=%async_computation | async-start | bytes 1572864 | tf_op jit(solution)/shard_map/all_to_all | solution.py:49
  27.2 0.0 all-reduce.2.cloned.1.call-start
  27.9 0.0 copy-done.1
  27.9 0.8 broadcast_select_fusion.1
  28.7 0.0 all-reduce.2.cloned.1.call-update
  28.7 0.0 copy-done.8
  28.7 0.0 copy-done.7
  28.8 0.1 copy.17
  28.9 0.1 eq.18
  29.0 0.2 fusion.5
  29.2 18.0 %all-to-all-done = bf16[192,1,2,1024]{3,2,1,0:T(2,128)(2,1)S(1)} async-done(((bf16[192,1,2,1024]{3,2,1,0:T(2,128)(2,1)}), bf16[192,1,2,1024]{3,2,1,0:T(2,128)(2,1)S(1)}, u32[]{:S(2)}, u32[]{:S(2)}) %all-to-all-start) | async-done | bytes 786464 | tf_op jit(solution)/shard_map/all_to_all | solution.py:49
  47.2 1.4 copy.21
  48.7 2.3 reshape.264
  51.0 174.9 %all-reduce.2.cloned.1.call-done = bf16[192,1024]{1,0:T(8,128)(2,1)} async-done(((bf16[192,1024]{1,0:T(8,128)(2,1)}), bf16[192,1024]{1,0:T(8,128)(2,1)}) %all-reduce.2.cloned.1.call-update) | async-done | bytes 393232 | tf_op jit(solution)/shard_map/psum | solution.py:16
  225.8 1.5 select_convert_fusion
  227.3 4.8 stack.3
  232.1 0.0 copy-start.6
  232.1 7.5 %all-to-all-start.1 = ((bf16[8,576,1024]{2,1,0:T(8,128)(2,1)}), bf16[8,576,1024]{2,1,0:T(8,128)(2,1)}, u32[]{:S(2)}, u32[]{:S(2)}) async-start(bf16[8,576,1024]{2,1,0:T(8,128)(2,1)} %stack.3), calls=%async_computation.1 | async-start | bytes 18874368 | tf_op jit(solution)/shard_map/all_to_all | solution.py:60
  239.6 0.0 copy-done.6
  239.7 0.1 iota_compare_fusion.2
  239.8 0.1 multiply_cosine_fusion.1
  239.9 0.4 multiply_cosine_fusion
  240.3 208.2 %all-to-all-done.1 = bf16[8,576,1024]{2,1,0:T(8,128)(2,1)} async-done(((bf16[8,576,1024]{2,1,0:T(8,128)(2,1)}), bf16[8,576,1024]{2,1,0:T(8,128)(2,1)}, u32[]{:S(2)}, u32[]{:S(2)}) %all-to-all-start.1) | async-done | bytes 9437216 | tf_op jit(solution)/shard_map/all_to_all | solution.py:60
  448.5 5.7 fusion
  454.2 0.1 slice.20
  454.3 12.7 %convert_bitcast_fusion = f32[8,72,8,1024]{3,2,1,0:T(8,128)} fusion(bf16[8,576,1024]{2,1,0:T(8,128)(2,1)} %all-to-all-done.1), kind=kLoop, calls=%fused_computation.1 | loop fusion | flops 4718592 | bytes 28311552
  466.9 7.8 %copy.25 = f32[8,72,8,1024]{3,2,0,1:T(8,128)S(1)} copy(f32[8,72,8,1024]{3,2,1,0:T(8,128)} %convert_bitcast_fusion) | data formatting | bytes 37748736 | tf_op jit(solution)/shard_map/convert_element_type | solution.py:61
  474.8 0.0 copy-start.5
  474.8 2.3 multiply_convert_fusion
  477.1 0.0 copy-start.2
  477.1 3.6 copy-done.2
  480.8 0.0 copy-done.5
  480.8 0.1 fusion.15
  480.9 250.1 %psum.15 = f32[4,1024]{1,0:T(4,128)S(1)} all-reduce(f32[4,1024]{1,0:T(4,128)S(1)} %fusion.15), channel_id=1, replica_groups=mesh['cfg'=64,'tp'=8] {'cfg'}, use_global_device_ids=true, to_apply=%region_3.4 | all-reduce | flops 4096 | bytes 32768 | tf_op jit(solution)/shard_map/psum | solution.py:77
  731.1 0.0 copy-start.3
  731.1 0.0 copy-start.9
  731.1 0.1 multiply_bitcast_fusion
  731.2 0.0 copy-done
  731.2 6.4 fusion.1
  737.6 0.0 copy-done.3
  737.6 0.4 copy-done.9
  738.0 2.6 convolution_multiply_fusion
  740.6 0.2 fusion.6
  740.8 0.1 pad_maximum_fusion
  740.9 0.0 copy-start.4
  740.9 0.1 subtract_convert_fusion.1
  741.0 0.3 fusion.20
  741.3 0.2 fusion.10
  741.5 0.2 fusion.4
  741.8 0.6 reshape.267
  742.4 0.0 copy-done.10
  742.4 0.0 copy-done.4
  (11 shorter events, 0.1 us)
Async XLA Ops:
  7.2 724.0 %copy-start = (bf16[8192,128]{1,0:T(8,128)(2,1)S(1)}, bf16[8192,128]{1,0:T(8,128)(2,1)}, u32[]{:S(2)}) copy-start(bf16[8192,128]{1,0:T(8,128)(2,1)} %param.13) | copy-start | bytes 6291460
  7.2 20.7 %copy-start.1 = (bf16[1,192,1024]{2,1,0:T(8,128)(2,1)S(1)}, bf16[1,192,1024]{2,1,0:T(8,128)(2,1)}, u32[]{:S(2)}) copy-start(bf16[1,192,1024]{2,1,0:T(8,128)(2,1)} %param.9) | copy-start | bytes 1179652
  7.2 21.5 %copy-start.8 = (s32[3,64]{1,0:T(4,128)S(1)}, s32[3,64]{1,0:T(4,128)}, u32[]{:S(2)}) copy-start(s32[3,64]{1,0:T(4,128)} %param.17) | copy-start | bytes 2308
  7.2 21.5 %copy-start.7 = (s32[3,64,2]{1,2,0:T(2,128)S(1)}, s32[3,64,2]{1,2,0:T(2,128)}, u32[]{:S(2)}) copy-start(s32[3,64,2]{1,2,0:T(2,128)} %param.16) | copy-start | bytes 4612
  16.9 30.4 %all-to-all-start = ((bf16[192,1,2,1024]{3,2,1,0:T(2,128)(2,1)}), bf16[192,1,2,1024]{3,2,1,0:T(2,128)(2,1)S(1)}, u32[]{:S(2)}, u32[]{:S(2)}) async-start(bf16[192,1,2,1024]{3,2,1,0:T(2,128)(2,1)} %broadcast_select_fusion), calls=%async_computation | async-start | bytes 1572864 | tf_op jit(solution)/shard_map/all_to_all | solution.py:49
  27.2 198.6 %all-reduce.2.cloned.1.call-start = ((), (), s32[]{:S(2)}) async-start(), calls=%async_computation.2 | async-start | bytes 786432 | tf_op jit(solution)/shard_map/psum | solution.py:16
  232.1 7.5 %copy-start.6 = (bf16[8192]{0:T(1024)(128)(2,1)S(1)}, bf16[8192]{0:T(1024)(128)(2,1)}, u32[]{:S(2)}) copy-start(bf16[8192]{0:T(1024)(128)(2,1)} %param.11) | copy-start | bytes 49156
  232.1 216.4 %all-to-all-start.1 = ((bf16[8,576,1024]{2,1,0:T(8,128)(2,1)}), bf16[8,576,1024]{2,1,0:T(8,128)(2,1)}, u32[]{:S(2)}, u32[]{:S(2)}) async-start(bf16[8,576,1024]{2,1,0:T(8,128)(2,1)} %stack.3), calls=%async_computation.1 | async-start | bytes 18874368 | tf_op jit(solution)/shard_map/all_to_all | solution.py:60
  474.8 6.0 copy-start.5
  477.1 3.6 copy-start.2
  731.1 6.5 copy-start.3
  731.1 7.0 copy-start.9
  738.0 4.4 copy-start.10
  740.9 1.5 copy-start.4
Sparse Core Ops, SparseCore 0:
  31.5 194.2 all-reduce.1
